TPU v7x, 32 devices: a whole 2x2x4 slice. The times are simulated.
32 devices in a mesh: dp: 8 (over y, x, core), ffn: 4 (over z).
Axes of the slice: x: 2, y: 2, z: 4, core: 2. Of those that a mesh axis runs over, the one named last changes fastest.
Arguments:
- text_hidden: bfloat16 [16384, 768], P(('dp', 'ffn')), may hold values from -6 to 6
- visual_maps: bfloat16 [1568, 2048], P(('dp', 'ffn')), may hold values from -1200 to 1200
- patch_order: int32 [32, 49], P(('dp', 'ffn')), may hold values from 0 to 48, each once within a row
- segment_ids: int32 [32, 561], P(('dp', 'ffn')), may hold values from 0 to 2, never falling along the last dimension, each value on 1 to 280 neighbouring positions
- rel_bucket: int32 [32, 561, 561], P(('dp', 'ffn')), may hold values from 0 to 31
- x_bucket: int32 [32, 561, 561], P(('dp', 'ffn')), may hold values from 0 to 63
- y_bucket: int32 [32, 561, 561], P(('dp', 'ffn')), may hold values from 0 to 63
- bn_scale: float32 [2048], replicated, may hold values from 0.1 to 1.9
- bn_shift: float32 [2048], replicated, may hold values from -3 to 3
- vis_proj: bfloat16 [2048, 768], P(('dp', 'ffn')), may hold values from -0.125 to 0.125
- w_query: bfloat16 [768, 768], P(('dp', 'ffn')), may hold values from -0.21875 to 0.21875
- w_key: bfloat16 [768, 768], P(('dp', 'ffn')), may hold values from -0.21875 to 0.21875
- w_value: bfloat16 [768, 768], P(('dp', 'ffn')), may hold values from -0.21875 to 0.21875
- w_output: bfloat16 [768, 768], P(('dp', 'ffn')), may hold values from -0.625 to 0.625
- rel_table: float32 [32, 12], replicated, may hold values from -4 to 4
- x_table: float32 [64, 12], replicated, may hold values from -4 to 4
- y_table: float32 [64, 12], replicated, may hold values from -4 to 4
- first_gain: float32 [768], replicated, may hold values from 0.1 to 1.9
- first_bias: float32 [768], replicated, may hold values from -2 to 2
- w_inner: bfloat16 [768, 3072], P('dp', 'ffn'), may hold values from -0.21875 to 0.21875
- b_inner: float32 [3072], replicated, may hold values from -2 to 2
- w_outer: bfloat16 [3072, 768], P('ffn', 'dp'), may hold values from -0.109375 to 0.109375
- b_outer: float32 [768], replicated, may hold values from -2 to 2
- second_gain: float32 [768], replicated, may hold values from 0.1 to 1.9
- second_bias: float32 [768], replicated, may hold values from -2 to 2
- cotangent: bfloat16 [17952, 768], P(('dp', 'ffn')), may hold values from -6 to 6
Outputs:
- output: bfloat16 [17952, 768], P(('dp', 'ffn'))
- text_grad: float32 [16384, 768], P(('dp', 'ffn'))
- visual_grad: float32 [1568, 2048], P(('dp', 'ffn'))
- bn_scale_grad: float32 [2048], replicated
- bn_shift_grad: float32 [2048], replicated
- vis_proj_grad: float32 [2048, 768], P(('dp', 'ffn'))
- w_query_grad: float32 [768, 768], P(('dp', 'ffn'))
- w_key_grad: float32 [768, 768], P(('dp', 'ffn'))
- w_value_grad: float32 [768, 768], P(('dp', 'ffn'))
- w_output_grad: float32 [768, 768], P(('dp', 'ffn'))
- rel_table_grad: float32 [32, 12], replicated
- x_table_grad: float32 [64, 12], replicated
- y_table_grad: float32 [64, 12], replicated
- first_gain_grad: float32 [768], replicated
- first_bias_grad: float32 [768], replicated
- w_inner_grad: float32 [768, 3072], P('dp', 'ffn')
- b_inner_grad: float32 [3072], replicated
- w_outer_grad: float32 [3072, 768], P('ffn', 'dp')
- b_outer_grad: float32 [768], replicated
- second_gain_grad: float32 [768], replicated
- second_bias_grad: float32 [768], replicated
Inputs may be any that keep to these rules, and one draw needn't show every extreme that they name: Each row of patch_order names every one of the 49 cells of its packed row once. `segment_ids`: document numbers never fall along a packed row.
All inputs are finite; a program needn't handle non-finite values.
Results may differ from a plain program's by a relative error of at most 0.019.
Values may be sent and summed in bfloat16 or wider, within the bound.
No kernel may reach another device: no remote copies, remote signals or barrier semaphores. Data moves between devices by JAX's collectives and lax.ppermute only.
A program may use at most 320 MiB of HBM per device.

v0:
```python
import jax
import jax.numpy as jnp
from jax import lax
from jax.sharding import PartitionSpec as P

EPS = 1e-05
NEG = -1e30
HIGH = lax.Precision.HIGHEST
BLOCK_ROWS = 192


def norm_layer(values, gain, bias):
    center = values - jnp.mean(values, -1, keepdims=True)
    spread = jnp.mean(center * center, -1, keepdims=True)
    return center * lax.rsqrt(spread + EPS) * gain + bias


def gelu_fn(values):
    return jax.nn.gelu(values, approximate=True)


def contract_last(left, right):
    return lax.dot_general(
        left, right, (((1,), (1,)), ((), ())), preferred_element_type=jnp.float32
    )


def contract_first(left, right):
    return lax.dot_general(
        left, right, (((0,), (0,)), ((), ())), preferred_element_type=jnp.float32
    )


def head_split(rows_in, heads):
    return rows_in.reshape(rows_in.shape[0], heads, rows_in.shape[1] // heads)


def one_hot_block(bucket, levels_count):
    levels = jnp.arange(levels_count, dtype=jnp.int32)
    return (bucket[:, :, None] == levels[None, None, :]).astype(jnp.float32)


def table_bias(table, bucket):
    length = bucket.shape[0]
    pieces = []
    for begin in range(0, length, BLOCK_ROWS):
        finish = min(begin + BLOCK_ROWS, length)
        onehot = one_hot_block(bucket[begin:finish], table.shape[0])
        pieces.append(jnp.einsum("ijb,bh->hij", onehot, table, precision=HIGH))
    return jnp.concatenate(pieces, 1)


def table_grad(bucket, grad_scores, levels_count):
    length = bucket.shape[0]
    total = jnp.zeros((levels_count, grad_scores.shape[0]), jnp.float32)
    for begin in range(0, length, BLOCK_ROWS):
        finish = min(begin + BLOCK_ROWS, length)
        onehot = one_hot_block(bucket[begin:finish], levels_count)
        total = total + jnp.einsum(
            "ijb,hij->bh", onehot, grad_scores[:, begin:finish], precision=HIGH
        )
    return total


def scores_of(query, key_rows, segment, bias, heads):
    scale = (query.shape[1] // heads) ** (-0.5)
    raw = jnp.einsum(
        "ihe,jhe->hij",
        head_split(query, heads),
        head_split(key_rows, heads),
        preferred_element_type=jnp.float32,
    )
    allowed = (segment[:, None] == segment[None, :])[None]
    return (jnp.where(allowed, raw * scale + bias, NEG), scale)


def forward_seq(items, heads):
    query, key_rows, value_rows, segment, bias = items
    scores, scale = scores_of(query, key_rows, segment, bias, heads)
    peak = jnp.max(scores, -1, keepdims=True)
    expo = jnp.exp(scores - peak)
    total = jnp.sum(expo, -1, keepdims=True)
    probs = (expo / total).astype(jnp.bfloat16)
    mixed = jnp.einsum(
        "hij,jhe->ihe", probs, head_split(value_rows, heads), preferred_element_type=jnp.float32
    )
    return (mixed.reshape(query.shape).astype(jnp.bfloat16), peak + jnp.log(total))


def backward_seq(carry, items, heads):
    query, key_rows, value_rows, segment, bias, logsum, grad_mixed, rel_ids, x_ids, y_ids = items
    scores, scale = scores_of(query, key_rows, segment, bias, heads)
    probs = jnp.exp(scores - logsum)
    grad_heads = head_split(grad_mixed, heads)
    grad_value = jnp.einsum(
        "hij,ihe->jhe", probs.astype(jnp.bfloat16), grad_heads, preferred_element_type=jnp.float32
    )
    grad_probs = jnp.einsum(
        "ihe,jhe->hij",
        grad_heads,
        head_split(value_rows, heads),
        preferred_element_type=jnp.float32,
    )
    grad_scores = probs * (grad_probs - jnp.sum(probs * grad_probs, -1, keepdims=True))
    carry = (
        carry[0] + table_grad(rel_ids, grad_scores, carry[0].shape[0]),
        carry[1] + table_grad(x_ids, grad_scores, carry[1].shape[0]),
        carry[2] + table_grad(y_ids, grad_scores, carry[2].shape[0]),
    )
    scaled = (grad_scores * scale).astype(jnp.bfloat16)
    grad_query = jnp.einsum(
        "hij,jhe->ihe", scaled, head_split(key_rows, heads), preferred_element_type=jnp.float32
    )
    grad_key = jnp.einsum(
        "hij,ihe->jhe", scaled, head_split(query, heads), preferred_element_type=jnp.float32
    )
    shape_out = query.shape
    return (
        carry,
        (
            grad_query.reshape(shape_out).astype(jnp.bfloat16),
            grad_key.reshape(shape_out).astype(jnp.bfloat16),
            grad_value.reshape(shape_out).astype(jnp.bfloat16),
        ),
    )


def on_device(
    text_hidden,
    visual_maps,
    patch_order,
    segment_ids,
    rel_bucket,
    x_bucket,
    y_bucket,
    bn_scale,
    bn_shift,
    vis_proj,
    w_query,
    w_key,
    w_value,
    w_output,
    rel_table,
    x_table,
    y_table,
    first_gain,
    first_bias,
    w_inner,
    b_inner,
    w_outer,
    b_outer,
    second_gain,
    second_bias,
    cotangent,
):
    heads = rel_table.shape[1]
    seqs, visual_len = patch_order.shape
    length = segment_ids.shape[1]
    text_len = length - visual_len
    width = w_query.shape[1]
    count = visual_maps.shape[0] * lax.axis_size(("dp", "ffn"))
    visual = visual_maps.astype(jnp.float32)
    average = lax.psum(jnp.sum(visual, 0), ("dp", "ffn")) / count
    center = visual - average
    spread = lax.psum(jnp.sum(center * center, 0), ("dp", "ffn")) / count
    inv_std = lax.rsqrt(spread + EPS)
    normalized = center * inv_std
    bn_rows = (normalized * bn_scale + bn_shift).astype(jnp.bfloat16)
    proj_full, query_full, key_full, value_full, output_full = (
        lax.all_gather(vis_proj, ("dp", "ffn"), axis=0, tiled=True),
        lax.all_gather(w_query, ("dp", "ffn"), axis=0, tiled=True),
        lax.all_gather(w_key, ("dp", "ffn"), axis=0, tiled=True),
        lax.all_gather(w_value, ("dp", "ffn"), axis=0, tiled=True),
        lax.all_gather(w_output, ("dp", "ffn"), axis=0, tiled=True),
    )
    tokens = jnp.dot(bn_rows, proj_full, preferred_element_type=jnp.float32).reshape(
        seqs, visual_len, width
    )
    picker = (
        patch_order[:, :, None] == jnp.arange(visual_len, dtype=jnp.int32)[None, None, :]
    ).astype(jnp.float32)
    tokens = jnp.einsum("sjc,scd->sjd", picker, tokens, precision=HIGH)
    hidden = jnp.concatenate(
        [text_hidden.astype(jnp.float32).reshape(seqs, text_len, width), tokens], 1
    )
    hidden = hidden.reshape(seqs * length, width)
    lowered = hidden.astype(jnp.bfloat16)
    query = jnp.dot(lowered, query_full, preferred_element_type=jnp.float32).astype(jnp.bfloat16)
    key_rows = jnp.dot(lowered, key_full, preferred_element_type=jnp.float32).astype(jnp.bfloat16)
    value_rows = jnp.dot(lowered, value_full, preferred_element_type=jnp.float32).astype(
        jnp.bfloat16
    )

    def bias_of(items):
        return (
            table_bias(rel_table, items[0])
            + table_bias(x_table, items[1])
            + table_bias(y_table, items[2])
        )

    biases = lax.map(bias_of, (rel_bucket, x_bucket, y_bucket))
    query_seq = query.reshape(seqs, length, width)
    key_seq = key_rows.reshape(seqs, length, width)
    value_seq = value_rows.reshape(seqs, length, width)

    def forward_item(items):
        return forward_seq(items, heads)

    mixed, logsum = lax.map(forward_item, (query_seq, key_seq, value_seq, segment_ids, biases))
    mixed = mixed.reshape(seqs * length, width)
    attended = jnp.dot(mixed, output_full, preferred_element_type=jnp.float32)
    first, first_pull = jax.vjp(norm_layer, hidden + attended, first_gain, first_bias)
    first_low = first.astype(jnp.bfloat16)
    inner_w, outer_w = (
        lax.all_gather(w_inner, "dp", axis=0, tiled=True),
        lax.all_gather(w_outer, "dp", axis=1, tiled=True),
    )
    position = lax.axis_index("ffn")
    columns = inner_w.shape[1]
    inner_bias = lax.dynamic_slice_in_dim(b_inner, position * columns, columns)
    all_rows = lax.all_gather(first_low, "ffn", axis=0, tiled=True)
    inner = jnp.dot(all_rows, inner_w, preferred_element_type=jnp.float32) + inner_bias
    gelu_out, gelu_pull = jax.vjp(gelu_fn, inner)
    activated = gelu_out.astype(jnp.bfloat16)
    outer = lax.psum_scatter(
        jnp.dot(activated, outer_w, preferred_element_type=jnp.float32).astype(jnp.bfloat16),
        "ffn",
        scatter_dimension=0,
        tiled=True,
    ).astype(jnp.float32)
    norm_out, second_pull = jax.vjp(norm_layer, first + outer + b_outer, second_gain, second_bias)
    output = norm_out.astype(jnp.bfloat16)
    grad_second, grad_gain_two, grad_bias_two = second_pull(cotangent.astype(jnp.float32))
    grad_outer_bias = jnp.sum(grad_second, 0)
    grad_low = grad_second.astype(jnp.bfloat16)
    grad_rows = lax.all_gather(grad_low, "ffn", axis=0, tiled=True)
    grad_act = contract_last(grad_rows, outer_w)
    grad_outer_w = contract_first(activated, grad_rows)
    (grad_inner,) = gelu_pull(grad_act)
    inner_total = jnp.sum(grad_inner, 0)
    grad_inner_low = grad_inner.astype(jnp.bfloat16)
    grad_inner_w = contract_first(all_rows, grad_inner_low)
    grad_first_ffn = lax.psum_scatter(
        contract_last(grad_inner_low, inner_w).astype(jnp.bfloat16),
        "ffn",
        scatter_dimension=0,
        tiled=True,
    ).astype(jnp.float32)
    grad_inner_bias = lax.dynamic_update_slice_in_dim(
        jnp.zeros_like(b_inner), inner_total, position * columns, 0
    )
    grad_inner_w, grad_outer_w = (
        lax.psum_scatter(
            grad_inner_w.astype(jnp.bfloat16), "dp", scatter_dimension=0, tiled=True
        ).astype(jnp.float32),
        lax.psum_scatter(
            grad_outer_w.astype(jnp.bfloat16), "dp", scatter_dimension=1, tiled=True
        ).astype(jnp.float32),
    )
    grad_attn, grad_gain_one, grad_bias_one = first_pull(grad_second + grad_first_ffn)
    grad_attn_low = grad_attn.astype(jnp.bfloat16)
    grad_output_w = contract_first(mixed, grad_attn_low)
    grad_mixed = contract_last(grad_attn_low, output_full).astype(jnp.bfloat16)
    zeros = (jnp.zeros_like(rel_table), jnp.zeros_like(x_table), jnp.zeros_like(y_table))

    def backward_item(carry, items):
        return backward_seq(carry, items, heads)

    tables_grad, grads_seq = lax.scan(
        backward_item,
        zeros,
        (
            query_seq,
            key_seq,
            value_seq,
            segment_ids,
            biases,
            logsum,
            grad_mixed.reshape(seqs, length, width),
            rel_bucket,
            x_bucket,
            y_bucket,
        ),
    )
    grad_query = grads_seq[0].reshape(seqs * length, width)
    grad_key = grads_seq[1].reshape(seqs * length, width)
    grad_value = grads_seq[2].reshape(seqs * length, width)
    grad_query_w = contract_first(lowered, grad_query)
    grad_key_w = contract_first(lowered, grad_key)
    grad_value_w = contract_first(lowered, grad_value)
    grad_hidden = (
        grad_attn
        + contract_last(grad_query, query_full)
        + contract_last(grad_key, key_full)
        + contract_last(grad_value, value_full)
    )
    grad_hidden = grad_hidden.reshape(seqs, length, width)
    text_grad = grad_hidden[:, :text_len].reshape(seqs * text_len, width)
    grad_tokens = jnp.einsum("sjc,sjd->scd", picker, grad_hidden[:, text_len:], precision=HIGH)
    grad_tokens = grad_tokens.reshape(seqs * visual_len, width).astype(jnp.bfloat16)
    grad_proj = contract_first(bn_rows, grad_tokens)
    grad_bn = contract_last(grad_tokens, proj_full)
    totals = lax.psum(
        (
            tables_grad[0],
            tables_grad[1],
            tables_grad[2],
            grad_gain_one,
            grad_bias_one,
            grad_inner_bias,
            grad_outer_bias,
            grad_gain_two,
            grad_bias_two,
            jnp.sum(grad_bn, 0),
            jnp.sum(grad_bn * normalized, 0),
        ),
        ("dp", "ffn"),
    )
    shift_grad = totals[9]
    scale_grad = totals[10]
    visual_grad = (
        bn_scale * inv_std * (grad_bn - shift_grad / count - normalized * scale_grad / count)
    )
    weight_grads = (
        lax.psum_scatter(grad_proj, ("dp", "ffn"), scatter_dimension=0, tiled=True),
        lax.psum_scatter(grad_query_w, ("dp", "ffn"), scatter_dimension=0, tiled=True),
        lax.psum_scatter(grad_key_w, ("dp", "ffn"), scatter_dimension=0, tiled=True),
        lax.psum_scatter(grad_value_w, ("dp", "ffn"), scatter_dimension=0, tiled=True),
        lax.psum_scatter(grad_output_w, ("dp", "ffn"), scatter_dimension=0, tiled=True),
    )
    return (
        output,
        text_grad,
        visual_grad,
        scale_grad,
        shift_grad,
        weight_grads[0],
        weight_grads[1],
        weight_grads[2],
        weight_grads[3],
        weight_grads[4],
        totals[0],
        totals[1],
        totals[2],
        totals[3],
        totals[4],
        grad_inner_w,
        totals[5],
        grad_outer_w,
        totals[6],
        totals[7],
        totals[8],
    )


def solution(mesh):
    return jax.shard_map(
        on_device,
        mesh=mesh,
        in_specs=(
            P(("dp", "ffn"), None),
            P(("dp", "ffn"), None),
            P(("dp", "ffn"), None),
            P(("dp", "ffn"), None),
            P(("dp", "ffn"), None, None),
            P(("dp", "ffn"), None, None),
            P(("dp", "ffn"), None, None),
            P(),
            P(),
            P(("dp", "ffn"), None),
            P(("dp", "ffn"), None),
            P(("dp", "ffn"), None),
            P(("dp", "ffn"), None),
            P(("dp", "ffn"), None),
            P(),
            P(),
            P(),
            P(),
            P(),
            P("dp", "ffn"),
            P(),
            P("ffn", "dp"),
            P(),
            P(),
            P(),
            P(("dp", "ffn"), None),
        ),
        out_specs=(
            P(("dp", "ffn"), None),
            P(("dp", "ffn"), None),
            P(("dp", "ffn"), None),
            P(),
            P(),
            P(("dp", "ffn"), None),
            P(("dp", "ffn"), None),
            P(("dp", "ffn"), None),
            P(("dp", "ffn"), None),
            P(("dp", "ffn"), None),
            P(),
            P(),
            P(),
            P(),
            P(),
            P("dp", "ffn"),
            P(),
            P("ffn", "dp"),
            P(),
            P(),
            P(),
        ),
        check_vma=False,
    )
```

profile of v0, /device:TPU:0, one launch (start us, length us, event | category | flops | bytes accessed | tf_op | source)
XLA Modules:
  0.0 1252.4 jit_solution(14479829655649892435)
XLA Ops:
  15.2 42.1 %psum.91 = f32[2048]{0:T(1024)S(1)} all-reduce(f32[2048]{0:T(1024)S(1)} %convert_reduce_fusion.1), channel_id=1, replica_groups=mesh['dp'=8,'ffn'=4] {'dp','ffn'}, use_global_device_ids=true, to_apply=%region_1.0 | all-reduce | flops 2048 | bytes 16384 | tf_op jit(solution)/shard_map/psum | solution.py:163
  57.5 40.5 %psum.92 = f32[2048]{0:T(1024)S(1)} all-reduce(f32[2048]{0:T(1024)S(1)} %fusion.140), channel_id=1, replica_groups=mesh['dp'=8,'ffn'=4] {'dp','ffn'}, use_global_device_ids=true, to_apply=%region_3.0 | all-reduce | flops 2048 | bytes 16384 | tf_op jit(solution)/shard_map/psum | solution.py:165
  195.0 13.3 %copy_bitcast_fusion = (f32[12,192,561]{2,1,0:T(8,128)}, f32[12,192,561]{2,1,0:T(8,128)}) fusion(f32[192,561,12]{1,2,0:T(8,128)} %fusion.3, f32[192,561,12]{1,2,0:T(8,128)} %fusion.5), kind=kLoop, calls=%fused_computation.78 | loop fusion | bytes 20680704 | tf_op jit(solution)/shard_map/while/body/eval_jaxpr/ijb,bh->hij/dot_general | solution.py:49
  208.3 13.5 %copy_bitcast_fusion.2 = (f32[12,192,561]{2,1,0:T(8,128)}, f32[12,192,561]{2,1,0:T(8,128)}) fusion(f32[192,561,12]{1,2,0:T(8,128)} %fusion.7, f32[192,561,12]{1,2,0:T(8,128)} %fusion.9), kind=kLoop, calls=%fused_computation.80 | loop fusion | bytes 20680704 | tf_op jit(solution)/shard_map/while/body/eval_jaxpr/ijb,bh->hij/dot_general | solution.py:49
  221.8 13.5 %copy_bitcast_fusion.4 = (f32[12,192,561]{2,1,0:T(8,128)}, f32[12,192,561]{2,1,0:T(8,128)}) fusion(f32[192,561,12]{1,2,0:T(8,128)} %fusion.26, f32[192,561,12]{1,2,0:T(8,128)} %fusion.28), kind=kLoop, calls=%fused_computation.82 | loop fusion | bytes 20680704 | tf_op jit(solution)/shard_map/while/body/eval_jaxpr/ijb,bh->hij/dot_general | solution.py:49
  265.5 26.3 %fusion.185 = (f32[12,561]{1,0:T(8,128)S(1)}, f32[12,561,561]{2,1,0:T(8,128)}) fusion(f32[12,177,561]{2,1,0:T(8,128)} %get-tuple-element.174, f32[12,192,561]{2,1,0:T(8,128)} %get-tuple-element.168, f32[12,192,561]{2,1,0:T(8,128)} %get-tuple-element.169, f32[12,177,561]{2,1,0:T(8,128)} %get-tuple-element.175, f32[12,192,561]{2,1,0:T(8,128)} %get-tuple-element.170, ...), kind=kOutput, calls=%fused_computation.226 | convolution fusion | flops 528724416 | bytes 62491472 | tf_op jit(solution)/shard_map/while/body/eval_jaxpr/ihe,jhe->hij/dot_general | solution.py:67
  316.5 67.7 %all-gather.26.cloned.1.call-done = bf16[4,561,768]{2,1,0:T(8,128)(2,1)} async-done(((bf16[1,561,768]{2,1,0:T(8,128)(2,1)}), bf16[4,561,768]{2,1,0:T(8,128)(2,1)}) %all-gather.26.cloned.1.call-update) | async-done | bytes 3446800 | tf_op jit(solution)/shard_map/all_gather | solution.py:221
  388.8 20.0 %all-gather.22.cloned.1.call-done = bf16[768,768]{1,0:T(8,128)(2,1)} async-done(((bf16[96,768]{1,0:T(8,128)(2,1)}), bf16[768,768]{1,0:T(8,128)(2,1)}) %all-gather.22.cloned.1.call-update) | async-done | bytes 1179664 | tf_op jit(solution)/shard_map/all_gather | solution.py:215
  416.8 17.9 %all-gather.24.cloned.1.call-done = bf16[768,768]{0,1:T(8,128)(2,1)} async-done(((bf16[768,96]{0,1:T(8,128)(2,1)}), bf16[768,768]{0,1:T(8,128)(2,1)}) %all-gather.24.cloned.1.call-update) | async-done | bytes 1179664 | tf_op jit(solution)/shard_map/all_gather | solution.py:216
  444.1 66.7 %fusion = bf16[568,768]{1,0:T(8,128)(2,1)S(1)} fusion(bf16[2244,768]{1,0:T(8,128)(2,1)} %convolution_convert_fusion.1), kind=kCustom, calls=%all-reduce-scatter | all-reduce-scatter fusion | flops 1744897 | bytes 4319744
  522.9 68.1 %all-gather.28.cloned.1.call-done = bf16[4,561,768]{2,1,0:T(8,128)(2,1)} async-done(((bf16[1,561,768]{2,1,0:T(8,128)(2,1)}), bf16[4,561,768]{2,1,0:T(8,128)(2,1)}) %all-gather.28.cloned.1.call-update) | async-done | bytes 3446800 | tf_op jit(solution)/shard_map/all_gather | solution.py:236
  627.6 65.0 %fusion.1 = bf16[568,768]{1,0:T(8,128)(2,1)} fusion(bf16[2244,768]{1,0:T(8,128)(2,1)} %convolution_convert_fusion), kind=kCustom, calls=%all-reduce-scatter.1 | all-reduce-scatter fusion | flops 1744897 | bytes 4319744
  727.0 15.4 %multiply_reduce_fusion = (f32[12,561]{1,0:T(8,128)S(1)}, f32[12,561,561]{2,1,0:T(8,128)}) fusion(f32[12,561,561]{2,1,0:T(8,128)} %get-tuple-element.160, f32[12,561]{1,0:T(8,128)S(1)} %log_add_fusion, bf16[561,12,64]{0,2,1:T(8,128)(2,1)S(1)} %bitcast.190, bf16[561,12,64]{0,2,1:T(8,128)(2,1)S(1)} %bitcast.203), kind=kOutput, calls=%fused_computation.24 | convolution fusion | flops 494734656 | bytes 31990464 | tf_op jit(solution)/shard_map/while/body/eval_jaxpr/ihe,jhe->hij/dot_general | solution.py:98
  742.9 18.8 %subtract_multiply_fusion = f32[12,561,561]{2,1,0:T(8,128)} fusion(f32[12,561,561]{2,1,0:T(8,128)} %get-tuple-element.164, f32[12,561,561]{2,1,0:T(8,128)} %get-tuple-element.160, f32[12,561]{1,0:T(8,128)S(1)} %get-tuple-element.163, f32[12,561]{1,0:T(8,128)S(1)} %log_add_fusion), kind=kLoop, calls=%fused_computation.23 | loop fusion | flops 11329956 | bytes 45373680 | tf_op jit(solution)/shard_map/while/body/eval_jaxpr/mul | solution.py:104
  843.1 14.9 %fusion.94 = f32[64,12]{0,1:T(8,128)S(1)} fusion(f32[12,177,561]{2,1,0:T(8,128)S(1)} %bitcast.188, s32[177,561]{1,0:T(8,128)S(1)} %bitcast.215), kind=kOutput, calls=%fused_computation.135 | convolution fusion | flops 921476160 | bytes 5166516 | tf_op jit(solution)/shard_map/while/body/eval_jaxpr/ijb,hij->bh/dot_general | solution.py:59
  858.0 14.5 %fusion.91 = f32[64,12]{0,1:T(8,128)S(1)} fusion(f32[12,177,561]{2,1,0:T(8,128)S(1)} %bitcast.188, s32[177,561]{1,0:T(8,128)S(1)} %bitcast.217), kind=kOutput, calls=%fused_computation.134 | convolution fusion | flops 921476160 | bytes 5166516 | tf_op jit(solution)/shard_map/while/body/eval_jaxpr/ijb,hij->bh/dot_general | solution.py:59
  872.6 17.8 %fusion.103 = f32[64,12]{0,1:T(8,128)S(1)} fusion(f32[12,192,561]{2,1,0:T(8,128)S(1)} %bitcast.186, s32[192,561]{1,0:T(8,128)S(1)} %bitcast.211), kind=kOutput, calls=%fused_computation.138 | convolution fusion | flops 999567360 | bytes 5604096 | tf_op jit(solution)/shard_map/while/body/eval_jaxpr/ijb,hij->bh/dot_general | solution.py:59
  890.4 17.8 %fusion.97 = f32[64,12]{0,1:T(8,128)S(1)} fusion(f32[12,192,561]{2,1,0:T(8,128)S(1)} %bitcast.186, s32[192,561]{1,0:T(8,128)S(1)} %bitcast.213), kind=kOutput, calls=%fused_computation.136 | convolution fusion | flops 999567360 | bytes 5604096 | tf_op jit(solution)/shard_map/while/body/eval_jaxpr/ijb,hij->bh/dot_general | solution.py:59
  908.2 18.4 %fusion.112 = f32[64,12]{0,1:T(8,128)S(1)} fusion(f32[64,12]{0,1:T(8,128)S(1)} %fusion.94, f32[64,12]{0,1:T(8,128)S(1)} %fusion.103, f32[12,192,561]{2,1,0:T(8,128)S(1)} %get-tuple-element.148, s32[192,561]{1,0:T(8,128)S(1)} %bitcast.207), kind=kOutput, calls=%fused_computation.141 | convolution fusion | flops 999568896 | bytes 5610240 | tf_op jit(solution)/shard_map/while/body/eval_jaxpr/ijb,hij->bh/dot_general | solution.py:59
  926.7 18.4 %fusion.118 = f32[64,12]{0,1:T(8,128)S(1)} fusion(f32[64,12]{0,1:T(8,128)S(1)} %fusion.91, f32[64,12]{0,1:T(8,128)S(1)} %fusion.97, f32[12,192,561]{2,1,0:T(8,128)S(1)} %get-tuple-element.148, s32[192,561]{1,0:T(8,128)S(1)} %bitcast.209), kind=kOutput, calls=%fused_computation.143 | convolution fusion | flops 999568896 | bytes 5610240 | tf_op jit(solution)/shard_map/while/body/eval_jaxpr/ijb,hij->bh/dot_general | solution.py:59
  945.2 43.8 %all-reduce.4 = (f32[2048]{0:T(1024)S(1)}, f32[2048]{0:T(1024)S(1)}, f32[32,12]{0,1:T(8,128)}, f32[64,12]{0,1:T(8,128)}, f32[64,12]{0,1:T(8,128)}, /*index=5*/f3...) all-reduce(f32[2048]{0:T(1024)S(1)} %get-tuple-element.111, ...), channel_id=1, replica_groups=mesh['dp'=8,'ffn'=4] {'dp','ffn'}, use_global_device_ids=true, to_apply=%region_20.21 | all-reduce | flops 12928 | bytes 103424 | tf_op jit(solution)/shard_map/psum | solution.py:303
  994.5 26.6 %reduce-scatter.14.cloned.1.call-done = f32[24,768]{1,0:T(8,128)} async-done(((f32[768,768]{1,0:T(8,128)}), f32[24,768]{1,0:T(8,128)}) %reduce-scatter.14.cloned.1.call-update) | async-done | bytes 73744 | tf_op jit(solution)/shard_map/reduce_scatter | solution.py:326
  1021.0 104.7 %reduce-scatter.16.cloned.1.call-done = f32[24,768]{1,0:T(8,128)} async-done(((f32[768,768]{1,0:T(8,128)}), f32[24,768]{1,0:T(8,128)}) %reduce-scatter.16.cloned.1.call-update) | async-done | bytes 73744 | tf_op jit(solution)/shard_map/reduce_scatter | solution.py:327
  1125.7 119.6 %reduce-scatter.12.cloned.1.call-done = f32[64,768]{1,0:T(8,128)} async-done(((f32[2048,768]{1,0:T(8,128)}), f32[64,768]{1,0:T(8,128)}) %reduce-scatter.12.cloned.1.call-update) | async-done | bytes 196624 | tf_op jit(solution)/shard_map/reduce_scatter | solution.py:325
  (325 shorter events, 350.6 us)
Async XLA Ops:
  7.2 240.8 %all-gather.12.cloned.1.call-start = ((), (), s32[]{:S(2)}) async-start(), calls=%async_computation.7 | async-start | bytes 3244032 | tf_op jit(solution)/shard_map/all_gather | solution.py:170
  8.0 243.6 %all-gather.16.cloned.1.call-start = ((), (), s32[]{:S(2)}) async-start(), calls=%async_computation.9 | async-start | bytes 1216512 | tf_op jit(solution)/shard_map/all_gather | solution.py:171
  8.7 246.3 %all-gather.18.cloned.1.call-start = ((), (), s32[]{:S(2)}) async-start(), calls=%async_computation.10 | async-start | bytes 1216512 | tf_op jit(solution)/shard_map/all_gather | solution.py:172
  9.4 251.0 %all-gather.14.cloned.1.call-start = ((), (), s32[]{:S(2)}) async-start(), calls=%async_computation.8 | async-start | bytes 1216512 | tf_op jit(solution)/shard_map/all_gather | solution.py:173
  10.0 299.4 %all-gather.20.cloned.1.call-start = ((), (), s32[]{:S(2)}) async-start(), calls=%async_computation.11 | async-start | bytes 1216512 | tf_op jit(solution)/shard_map/all_gather | solution.py:174
  10.6 373.6 %all-gather.26.cloned.1.call-start = ((), (), s32[]{:S(2)}) async-start(), calls=%async_computation.21 | async-start | bytes 4362240 | tf_op jit(solution)/shard_map/all_gather | solution.py:221
  57.4 190.6 %copy-start.45 = (f32[2048]{0:T(1024)}, f32[2048]{0:T(1024)S(1)}, u32[]{:S(2)}) copy-start(f32[2048]{0:T(1024)S(1)} %broadcast_multiply_fusion.1) | copy-start | bytes 24580
  314.1 94.6 %all-gather.22.cloned.1.call-start = ((), (), s32[]{:S(2)}) async-start(), calls=%async_computation.12 | async-start | bytes 1327104 | tf_op jit(solution)/shard_map/all_gather | solution.py:215
  314.9 119.8 %all-gather.24.cloned.1.call-start = ((), (), s32[]{:S(2)}) async-start(), calls=%async_computation.13 | async-start | bytes 1327104 | tf_op jit(solution)/shard_map/all_gather | solution.py:216
  315.7 275.4 %all-gather.28.cloned.1.call-start = ((), (), s32[]{:S(2)}) async-start(), calls=%async_computation.22 | async-start | bytes 4362240 | tf_op jit(solution)/shard_map/all_gather | solution.py:236
  316.5 118.2 %copy-start.73 = (f32[768]{0:T(1024)}, f32[768]{0:T(1024)S(1)}, u32[]{:S(2)}) copy-start(f32[768]{0:T(1024)S(1)} %dynamic_slice.44) | copy-start | bytes 9220
  416.8 95.9 %copy-start.79 = (u32[32]{0:T(128)S(1)}, u32[32]{0:T(128)}, u32[]{:S(2)}) copy-start(u32[32]{0:T(128)} %constant.126) | copy-start | bytes 388
  510.8 3.1 collective-permute-start
  522.6 468.5 %reduce-scatter.24.cloned.1.call-start = ((), (), s32[]{:S(2)}) async-start(), calls=%async_computation.20 | async-start | bytes 1327104 | tf_op jit(solution)/shard_map/reduce_scatter | solution.py:256
  604.3 388.5 %reduce-scatter.22.cloned.1.call-start = ((), (), s32[]{:S(2)}) async-start(), calls=%async_computation.19 | async-start | bytes 1327104 | tf_op jit(solution)/shard_map/reduce_scatter | solution.py:253
  620.4 374.1 %reduce-scatter.20.cloned.1.call-start = ((), (), s32[]{:S(2)}) async-start(), calls=%async_computation.18 | async-start | bytes 2433024 | tf_op jit(solution)/shard_map/reduce_scatter | solution.py:329
  693.4 3.5 collective-permute-start.1
  712.9 281.6 %reduce-scatter.18.cloned.1.call-start = ((), (), s32[]{:S(2)}) async-start(), calls=%async_computation.17 | async-start | bytes 2433024 | tf_op jit(solution)/shard_map/reduce_scatter | solution.py:328
  742.4 278.6 %reduce-scatter.14.cloned.1.call-start = ((), (), s32[]{:S(2)}) async-start(), calls=%async_computation.15 | async-start | bytes 2433024 | tf_op jit(solution)/shard_map/reduce_scatter | solution.py:326
  773.1 352.6 %reduce-scatter.16.cloned.1.call-start = ((), (), s32[]{:S(2)}) async-start(), calls=%async_computation.16 | async-start | bytes 2433024 | tf_op jit(solution)/shard_map/reduce_scatter | solution.py:327
  784.7 460.7 %reduce-scatter.12.cloned.1.call-start = ((), (), s32[]{:S(2)}) async-start(), calls=%async_computation.14 | async-start | bytes 6488064 | tf_op jit(solution)/shard_map/reduce_scatter | solution.py:325
  908.2 337.1 %copy-start.1 = (f32[64,12]{0,1:T(8,128)S(1)}, f32[64,12]{0,1:T(8,128)}, u32[]{:S(2)}) copy-start(f32[64,12]{0,1:T(8,128)} %param.42) | copy-start | bytes 9220
  989.0 256.3 %copy-start.70 = (f32[2048]{0:T(1024)}, f32[2048]{0:T(1024)S(1)}, u32[]{:S(2)}) copy-start(f32[2048]{0:T(1024)S(1)} %get-tuple-element.112) | copy-start | bytes 24580
  989.0 256.3 %copy-start.71 = (f32[2048]{0:T(1024)}, f32[2048]{0:T(1024)S(1)}, u32[]{:S(2)}) copy-start(f32[2048]{0:T(1024)S(1)} %get-tuple-element.113) | copy-start | bytes 24580
  (83 other events, 1237.6 us)
Sparse Core Ops, SparseCore 0:
  10.9 61.6 all-gather.11
  75.4 52.9 all-gather.15
  131.3 53.0 all-gather.17
  187.0 53.0 all-gather.13
  242.7 53.0 all-gather.19
  314.3 69.8 all-gather.25
  386.0 22.6 all-gather.21
  410.6 24.0 all-gather.23
  522.8 68.1 all-gather.27
  604.4 35.3 reduce-scatter.23
  643.4 36.7 reduce-scatter.21
  713.0 99.2 reduce-scatter.19
  819.1 98.0 reduce-scatter.17
  922.9 98.0 reduce-scatter.13
  1027.6 98.0 reduce-scatter.15
  1131.8 113.5 reduce-scatter.11
where the time goes:
time: 1260 us; the launch traced here: 1250 us
  waiting for transfers between devices  430 us (34%)
  matrix products  381 us (30%)
  blocking collectives  258 us (20%)
  local copies, waits for them, and re-layouts  111 us (9%)
  other arithmetic  49.4 us (4%)
  between operations  16.4 us (1%)
    dot_general x9, matrix products, table_grad(): jnp.einsum('ijb,hij->bh', onehot, grad_scores[:, begin:finish], precision...  133 us
    unnamed x2, blocking collectives  132 us
    reduce_scatter x1, waiting for transfers between devices, on_device(): lax.psum_scatter(grad_proj, ('dp', 'ffn'), scatter_dimension=0, tiled=True)  120 us
    reduce_scatter x1, waiting for transfers between devices, on_device(): lax.psum_scatter(grad_key_w, ('dp', 'ffn'), scatter_dimension=0, tiled=True)  105 us
    dot_general x9, matrix products, table_bias(): pieces.append(jnp.einsum('ijb,bh->hij', onehot, table, precision=HIGH))  87.6 us
    all_gather x1, waiting for transfers between devices, on_device(): grad_rows = lax.all_gather(grad_low, 'ffn', axis=0, tiled=True)  68.1 us
    all_gather x1, waiting for transfers between devices, on_device(): all_rows = lax.all_gather(first_low, 'ffn', axis=0, tiled=True)  67.7 us
    dot_general x5, local copies, waits for them, and re-layouts, table_bias(): pieces.append(jnp.einsum('ijb,bh->hij', onehot, table, precision=HIGH))  57.1 us
  transfers between devices with their start and end apart: 18, of which 8 were waited for; matrix products, arithmetic and copies ran while one was open for 45% of the time, Pallas kernels for 0%

commit v1 on v0

v1 whole, which is shorter than its diff:
```python
import functools

import jax
import jax.numpy as jnp
from jax import lax
from jax.experimental import pallas as pl
from jax.experimental.pallas import tpu as pltpu
from jax.sharding import PartitionSpec as P

EPS = 1e-05
NEG = -1e30
F32 = jnp.float32
BF16 = jnp.bfloat16
ALL = ("dp", "ffn")
LEVELS = 21845.0
MIB = 2**20


def dot_nn(a, b):
    return lax.dot_general(a, b, (((1,), (0,)), ((), ())), preferred_element_type=F32)


def dot_nt(a, b):
    return lax.dot_general(a, b, (((1,), (1,)), ((), ())), preferred_element_type=F32)


def dot_tn(a, b):
    return lax.dot_general(a, b, (((0,), (0,)), ((), ())), preferred_element_type=F32)


def pad_rows(values, rows):
    return jnp.pad(values, ((0, rows - values.shape[0]), (0, 0)))


def send_dp(values, bits):
    size = lax.axis_size("dp")
    return lax.ppermute(values, "dp", [(i, i ^ bits) for i in range(size)])


def send_ffn(values, shift):
    size = lax.axis_size("ffn")
    return lax.ppermute(values, "ffn", [(i, (i + shift) % size) for i in range(size)])


def swap_ffn(values, bits):
    size = lax.axis_size("ffn")
    return lax.ppermute(values, "ffn", [(i, i ^ bits) for i in range(size)])


def exchanges():
    steps = []
    bit = 1
    while bit < lax.axis_size("dp"):
        steps.append(functools.partial(send_dp, bits=bit))
        bit *= 2
    bit = 1
    while bit < lax.axis_size("ffn"):
        steps.append(functools.partial(swap_ffn, bits=bit))
        bit *= 2
    return steps


def sum_all(values):
    for step in exchanges():
        values = values + step(values)
    return values


def moments_all(mean, spread, rows):
    pack = jnp.stack([mean, spread])
    for step in exchanges():
        other = step(pack)
        gap = pack[0] - other[0]
        pack = jnp.stack(
            [(pack[0] + other[0]) * 0.5, pack[1] + other[1] + gap * gap * (rows * 0.5)]
        )
        rows = rows * 2
    return pack[0], pack[1] / rows


def gather_ffn(shard):
    size = lax.axis_size("ffn")
    here = lax.axis_index("ffn")
    parts = [shard] + [send_ffn(shard, k) for k in range(1, size)]
    slots = []
    for slot in range(size):
        value = parts[0]
        for k in range(1, size):
            value = jnp.where((here - k + size) % size == slot, parts[k], value)
        slots.append(value)
    return jnp.stack(slots)


def gather_quads(block):
    quads = lax.axis_size("dp") // 2
    if quads != 4:
        return [block] + [send_dp(block, 2 * k) for k in range(1, quads)]
    half = block.shape[0] // 2
    from_x = send_dp(block, 2)
    from_y = send_dp(block, 4)
    low = send_dp(from_x[:half], 4)
    high = send_dp(from_y[half:], 2)
    return [block, from_x, from_y, (low, high)]


def scatter_all(blocks):
    quads = lax.axis_size("dp") // 2
    size = lax.axis_size("ffn")
    place = lax.axis_index("dp")
    core, quad = place % 2, place // 2
    here = lax.axis_index("ffn")
    blocks = blocks.reshape((quads, 2) + blocks.shape[1:])
    away = lax.dynamic_index_in_dim(blocks, 1 - core, 1, keepdims=False)
    mine = lax.dynamic_index_in_dim(blocks, core, 1, keepdims=False)
    mine = (mine.astype(F32) + send_dp(away, 1).astype(F32)).astype(BF16)

    def of_quad(k):
        return lax.dynamic_index_in_dim(mine, quad ^ k, 0, keepdims=False)

    if quads == 4:
        own, to_x, to_y, diag = [of_quad(k) for k in range(4)]
        half = diag.shape[1] // 2
        low = send_dp(diag[:, :half], 4)
        high = send_dp(diag[:, half:], 2)
        to_x = jnp.concatenate(
            [(to_x[:, :half].astype(F32) + low.astype(F32)).astype(BF16), to_x[:, half:]], 1
        )
        to_y = jnp.concatenate(
            [to_y[:, :half], (to_y[:, half:].astype(F32) + high.astype(F32)).astype(BF16)], 1
        )
        own = own.astype(F32) + send_dp(to_x, 2).astype(F32) + send_dp(to_y, 4).astype(F32)
    else:
        own = of_quad(0).astype(F32)
        for k in range(1, quads):
            own = own + send_dp(of_quad(k), 2 * k).astype(F32)
    total = lax.dynamic_index_in_dim(own, here, 0, keepdims=False)
    own = own.astype(BF16)
    for k in range(1, size):
        piece = lax.dynamic_index_in_dim(own, (here + k) % size, 0, keepdims=False)
        total = total + send_ffn(piece, k).astype(F32)
    return total


def place_kernel(layout, place_ref, *refs):
    count = len(layout)
    parts = refs[: -count - 1]
    outs = refs[-count - 1 : -1]
    sems = refs[-1]
    copies = []
    for n, pieces in enumerate(parts):
        device = place_ref[n]
        for m, (begin, rows) in enumerate(layout):
            copy = pltpu.make_async_copy(
                pieces.at[pl.ds(begin, rows), :],
                outs[m].at[pl.ds(pl.multiple_of(device * rows, 16), rows), :],
                sems.at[n, m],
            )
            copy.start()
            copies.append(copy)
    for copy in copies:
        copy.wait()


def place_blocks(parts, places, layout):
    width = parts[0].shape[1]
    count = len(parts)
    return pl.pallas_call(
        functools.partial(place_kernel, layout),
        in_specs=[pl.BlockSpec(memory_space=pltpu.SMEM)]
        + [pl.BlockSpec(memory_space=pl.ANY)] * count,
        out_specs=[pl.BlockSpec(memory_space=pl.ANY)] * len(layout),
        out_shape=[jax.ShapeDtypeStruct((rows * count, width), BF16) for _, rows in layout],
        scratch_shapes=[pltpu.SemaphoreType.DMA((count, len(layout)))],
        name="place_blocks",
    )(places, *parts)


def bias_kernel(rows_step, rel_ref, x_ref, y_ref, tab_ref, out_ref):
    pairs = out_ref.shape[0]
    both = [jnp.broadcast_to(tab_ref[p : p + 1, :], (8, 128)) for p in range(pairs)]
    rel = [jnp.broadcast_to(tab_ref[8 + p : 9 + p, :], (8, 128)) for p in range(pairs)]

    def pick(table, index):
        return jnp.take_along_axis(table, index, axis=1, mode="promise_in_bounds")

    for c in range(out_ref.shape[2] // 128):
        for r in range(rows_step // 8):
            rows, cols = pl.ds(r * 8, 8), pl.ds(c * 128, 128)
            rel_id = rel_ref[0, rows, cols] & 31
            x_id = x_ref[0, rows, cols] & 63
            y_id = (y_ref[0, rows, cols] & 63) + 64
            for p in range(pairs):
                out_ref[p, rows, cols] = (
                    pick(rel[p], rel_id) + pick(both[p], x_id) + pick(both[p], y_id)
                )


def bias_words(rel, x, y, table, rows, pairs):
    step = 64
    lanes = pl.cdiv(rows, 128) * 128
    ids = pl.BlockSpec((1, step, lanes), lambda i: (0, i, 0))
    return pl.pallas_call(
        functools.partial(bias_kernel, step),
        grid=(rows // step,),
        in_specs=[ids, ids, ids, pl.BlockSpec(table.shape, lambda i: (0, 0))],
        out_specs=pl.BlockSpec((pairs, step, lanes), lambda i: (0, i, 0)),
        out_shape=jax.ShapeDtypeStruct((pairs, rows, lanes), jnp.int32),
        compiler_params=pltpu.CompilerParams(vmem_limit_bytes=40 * MIB),
        cost_estimate=pl.CostEstimate(flops=0, bytes_accessed=60_000_000, transcendentals=0),
        name="bias_words",
    )(rel, x, y, table)


def lane_halves(rows):
    lane = lax.broadcasted_iota(jnp.int32, (rows, 128), 1)
    return lane < 64, lane >= 64


def attend_kernel(unit_ref, q_ref, k_ref, v_ref, w_ref, col_ref, row_ref, p_ref, o_ref, mask_ref):
    @pl.when(pl.program_id(0) == 0)
    def _():
        mask_ref[...] = jnp.where(col_ref[...] == row_ref[...], 0.0, NEG)

    unit = unit_ref[0]
    rows = q_ref.shape[0]
    halves = lane_halves(rows)
    q, k, v = q_ref[...], k_ref[...], v_ref[...]
    none = jnp.zeros_like(q)
    words = w_ref[0][:, :rows]
    mask = mask_ref[...]
    mixed = jnp.zeros((rows, 128), F32)
    for h in range(2):
        scores = dot_nt(jnp.where(halves[h], q, none), k)
        word = (words & 0xFFFF) if h == 0 else lax.shift_right_logical(words, 16)
        scores = scores + word.astype(F32) * unit + mask
        expo = jnp.exp(scores - jnp.max(scores, -1, keepdims=True))
        probs = (expo * (1.0 / jnp.sum(expo, -1, keepdims=True))).astype(BF16)
        p_ref[h] = probs
        mixed = mixed + dot_nn(probs, jnp.where(halves[h], v, none))
    o_ref[...] = mixed.astype(BF16)


def attend(unit, qkv, words, segments):
    pairs = words.shape[0]
    rows = qkv.shape[0]
    col = [pl.BlockSpec((rows, 128), lambda p, n=n: (0, n * pairs + p)) for n in range(3)]
    flops = pairs * 4 * 2 * rows * rows * 128
    return pl.pallas_call(
        attend_kernel,
        grid=(pairs,),
        in_specs=[
            pl.BlockSpec(memory_space=pltpu.SMEM),
            col[0],
            col[1],
            col[2],
            pl.BlockSpec((1,) + words.shape[1:], lambda p: (p, 0, 0)),
            pl.BlockSpec((rows, 1), lambda p: (0, 0)),
            pl.BlockSpec((1, rows), lambda p: (0, 0)),
        ],
        out_specs=[
            pl.BlockSpec((2, rows, rows), lambda p: (p, 0, 0)),
            pl.BlockSpec((rows, 128), lambda p: (0, p)),
        ],
        out_shape=[
            jax.ShapeDtypeStruct((2 * pairs, rows, rows), BF16),
            jax.ShapeDtypeStruct((rows, pairs * 128), BF16),
        ],
        scratch_shapes=[pltpu.VMEM((rows, rows), F32)],
        compiler_params=pltpu.CompilerParams(vmem_limit_bytes=50 * MIB),
        cost_estimate=pl.CostEstimate(flops=flops, bytes_accessed=40_000_000, transcendentals=0),
        name="attend",
    )(unit, qkv, qkv, qkv, words, segments[:, None], segments[None, :])


def attend_back_kernel(q_ref, k_ref, v_ref, g_ref, p_ref, ds_ref, dq_ref, dk_ref, dv_ref):
    rows = q_ref.shape[0]
    halves = lane_halves(rows)
    q, k, v, g = q_ref[...], k_ref[...], v_ref[...], g_ref[...]
    none = jnp.zeros_like(q)
    blank = jnp.zeros((rows, ds_ref.shape[2] - rows), BF16)
    dq = jnp.zeros((rows, 128), F32)
    dk, dv = dq, dq
    for h in range(2):
        low = p_ref[h]
        probs = low.astype(F32)
        weighted = probs * dot_nt(g, jnp.where(halves[h], v, none))
        ds = (weighted - probs * jnp.sum(weighted, -1, keepdims=True)).astype(BF16)
        ds_ref[h] = jnp.concatenate([ds, blank], 1)
        dq = dq + dot_nn(ds, jnp.where(halves[h], k, none))
        dv = dv + dot_tn(low, jnp.where(halves[h], g, none))
        dk = dk + dot_tn(ds, jnp.where(halves[h], q, none))
    dq_ref[...] = (dq * 0.125).astype(BF16)
    dk_ref[...] = dk.astype(BF16)
    dv_ref[...] = dv.astype(BF16)


def attend_back(qkv, grad, probs):
    pairs = probs.shape[0] // 2
    rows = qkv.shape[0]
    col = [pl.BlockSpec((rows, 128), lambda p, n=n: (0, n * pairs + p)) for n in range(3)]
    big = pl.BlockSpec((2, rows, rows), lambda p: (p, 0, 0))
    lanes = pl.cdiv(rows, 128) * 128
    out = jax.ShapeDtypeStruct(grad.shape, BF16)
    flops = pairs * 2 * 4 * 2 * rows * rows * 128
    return pl.pallas_call(
        attend_back_kernel,
        grid=(pairs,),
        in_specs=[col[0], col[1], col[2], col[0], big],
        out_specs=[pl.BlockSpec((2, rows, lanes), lambda p: (p, 0, 0)), col[0], col[0], col[0]],
        out_shape=[jax.ShapeDtypeStruct((2 * pairs, rows, lanes), BF16), out, out, out],
        compiler_params=pltpu.CompilerParams(vmem_limit_bytes=50 * MIB),
        cost_estimate=pl.CostEstimate(flops=flops, bytes_accessed=40_000_000, transcendentals=0),
        name="attend_back",
    )(qkv, qkv, qkv, grad, probs)


def table_kernel(length, step, levels, rel_ref, x_ref, y_ref, ds_ref, out_ref, rows_ref):
    place = pl.program_id(0)

    @pl.when(place == 0)
    def _():
        out_ref[...] = jnp.zeros_like(out_ref)
        rows_ref[...] = jnp.zeros_like(rows_ref)

    heads = ds_ref.shape[0]
    width = rel_ref.shape[2]
    level = [
        lax.broadcasted_iota(jnp.int32, (16, width), 0).astype(F32).astype(BF16) + BF16(16 * t)
        for t in range(max(levels) // 16)
    ]
    one = jnp.ones((16, width), BF16)
    none = jnp.zeros((16, width), BF16)

    def one_hot(ids, count):
        wide = jnp.broadcast_to(ids.astype(F32), (16, width)).astype(BF16)
        return [jnp.where(wide == level[t], one, none) for t in range(count // 16)]

    def body(r, _):
        for h in range(heads):
            values = ds_ref[h, pl.ds(pl.multiple_of(r * 16, 16), 16), :].astype(F32)
            for c in range(width // 128):
                rows_ref[c, pl.ds(h, 16, stride=16), :] = values[:, 128 * c : 128 * c + 128]
        total = out_ref[...]
        for n in range(16):
            grads = jnp.concatenate(
                [rows_ref[c, 16 * n : 16 * n + 16, :].astype(BF16) for c in range(width // 128)], 1
            )
            row = pl.ds(r * 16 + n, 1)
            hot = jnp.concatenate(
                one_hot(rel_ref[0, row, :], levels[0])
                + one_hot(x_ref[0, row, :], levels[1])
                + one_hot(y_ref[0, row, :], levels[2]),
                0,
            )
            total = total + dot_nt(hot, grads)
        out_ref[...] = total
        return 0

    left = length - place * step
    lax.fori_loop(0, jnp.minimum(step // 16, (left + 15) // 16), body, 0)


def table_sums(rel, x, y, ds, levels):
    step = 64
    length = rel.shape[1]
    heads, rows, lanes = ds.shape
    ids = pl.BlockSpec((1, step, lanes), lambda i: (0, i, 0))
    return pl.pallas_call(
        functools.partial(table_kernel, length, step, levels),
        grid=(rows // step,),
        in_specs=[ids, ids, ids, pl.BlockSpec((heads, step, lanes), lambda i: (0, i, 0))],
        out_specs=pl.BlockSpec((sum(levels), 16), lambda i: (0, 0)),
        out_shape=jax.ShapeDtypeStruct((sum(levels), 16), F32),
        scratch_shapes=[pltpu.VMEM((lanes // 128, 256, 128), F32)],
        compiler_params=pltpu.CompilerParams(vmem_limit_bytes=40 * MIB),
        cost_estimate=pl.CostEstimate(flops=0, bytes_accessed=120_000_000, transcendentals=0),
        name="table_sums",
    )(rel, x, y, ds)


def norm_stats(values):
    center = values - jnp.mean(values, -1, keepdims=True)
    scale = lax.rsqrt(jnp.mean(center * center, -1, keepdims=True) + EPS)
    return center * scale, scale


def norm_back(grad, normed, scale, gain):
    scaled = grad * gain
    return scale * (
        scaled
        - jnp.mean(scaled, -1, keepdims=True)
        - normed * jnp.mean(scaled * normed, -1, keepdims=True)
    )


def packed_tables(tables):
    top = functools.reduce(jnp.maximum, [jnp.max(jnp.abs(t)) for t in tables])
    top = jnp.maximum(top, 1e-30)
    words = []
    for table in tables:
        level = jnp.round((table / top + 1.0) * (0.5 * LEVELS)).astype(jnp.int32)
        level = level.reshape(table.shape[0], -1, 2)
        words.append((level[:, :, 0] + level[:, :, 1] * 65536).T)
    rel, x, y = words
    pairs = rel.shape[0]
    both = jnp.concatenate([x, y], 1)
    rel = jnp.pad(rel, ((0, 8 - pairs), (0, 128 - rel.shape[1])))
    return jnp.concatenate([jnp.pad(both, ((0, 8 - pairs), (0, 0))), rel]), (
        top * (2.0 / LEVELS)
    ).reshape(1)


def on_device(
    text_hidden,
    visual_maps,
    patch_order,
    segment_ids,
    rel_bucket,
    x_bucket,
    y_bucket,
    bn_scale,
    bn_shift,
    vis_proj,
    w_query,
    w_key,
    w_value,
    w_output,
    rel_table,
    x_table,
    y_table,
    first_gain,
    first_bias,
    w_inner,
    b_inner,
    w_outer,
    b_outer,
    second_gain,
    second_bias,
    cotangent,
):
    heads = rel_table.shape[1]
    pairs = heads // 2
    visual_len = patch_order.shape[1]
    length = segment_ids.shape[1]
    text_len = length - visual_len
    width = w_query.shape[1]
    dp, ffn = lax.axis_size("dp"), lax.axis_size("ffn")
    place, here = lax.axis_index("dp"), lax.axis_index("ffn")
    devices = dp * ffn
    rows = pl.cdiv(length, 64) * 64
    count = visual_maps.shape[0] * devices
    levels = (rel_table.shape[0], x_table.shape[0], y_table.shape[0])

    late = [w_inner.reshape(-1, width), w_outer.T.reshape(-1, width), w_output]
    late_rows = late[0].shape[0]
    late = jnp.concatenate(late, 0)
    late = lax.all_gather(late, ALL, axis=0).reshape((dp, ffn) + late.shape)

    shards = [w_query, w_key, w_value, vis_proj]
    near = gather_ffn(jnp.concatenate(shards, 0))
    begin = 0
    stacked = []
    layout = []
    for shard in shards:
        size = shard.shape[0]
        stacked.append(near[:, begin : begin + size].reshape(ffn * size, width))
        layout.append((begin * ffn, ffn * size))
        begin += size
    near = jnp.concatenate(stacked, 0)
    quads = gather_quads(near)
    parts, places = [], []
    for k, block in enumerate(quads):
        if isinstance(block, tuple):
            mine = jnp.concatenate(block, 0)
            other = jnp.concatenate([send_dp(piece, 1) for piece in block], 0)
        else:
            mine, other = block, send_dp(block, 1)
        parts += [mine, other]
        places += [place ^ (2 * k), place ^ (2 * k) ^ 1]
    query_full, key_full, value_full, proj_full = place_blocks(
        parts, jnp.stack(places).astype(jnp.int32), layout
    )

    table_words, unit = packed_tables((rel_table, x_table, y_table))
    words = bias_words(rel_bucket, x_bucket, y_bucket, table_words, rows, pairs)

    visual = visual_maps.astype(F32)
    local_mean = jnp.mean(visual, 0)
    local_spread = jnp.sum((visual - local_mean) ** 2, 0)
    average, spread = moments_all(local_mean, local_spread, visual_maps.shape[0])
    inv_std = lax.rsqrt(spread + EPS)
    normalized = (visual - average) * inv_std
    bn_rows = (normalized * bn_scale + bn_shift).astype(BF16)
    tokens = dot_nn(bn_rows, proj_full)
    picker = (patch_order[0][:, None] == jnp.arange(visual_len, dtype=jnp.int32)[None, :]).astype(
        F32
    )
    tokens = jnp.dot(picker, tokens, precision=lax.Precision.HIGHEST)
    hidden = pad_rows(jnp.concatenate([text_hidden.astype(F32), tokens], 0), rows)
    lowered = hidden.astype(BF16)
    qkv_full = jnp.concatenate([query_full, key_full, value_full], 1)
    qkv = dot_nn(lowered, qkv_full)
    qkv = jnp.concatenate([qkv[:, :width] * 0.125, qkv[:, width:]], 1).astype(BF16)

    segments = jnp.pad(segment_ids[0], (0, rows - length), constant_values=-1)
    probs, mixed = attend(unit, qkv, words, segments)

    inner_rows = w_inner.shape[0]
    columns = w_inner.shape[1]
    output_full = late[:, :, 2 * late_rows :].reshape(width, width)
    inner_w, outer_w = [
        late[:, :, n * late_rows : (n + 1) * late_rows]
        .reshape(dp, ffn, inner_rows, columns)
        .transpose(1, 0, 2, 3)
        .reshape(ffn, width, columns)
        for n in range(2)
    ]
    attended = dot_nn(mixed, output_full)
    first_n, first_r = norm_stats(hidden + attended)
    first = first_n * first_gain + first_bias
    first_low = first.astype(BF16)

    outer = first + b_outer
    acts, slopes = [], []
    for f in range(ffn):
        inner = dot_nn(first_low, inner_w[f]) + b_inner[f * columns : (f + 1) * columns]
        act, pull = jax.vjp(functools.partial(jax.nn.gelu, approximate=True), inner)
        acts.append(act.astype(BF16))
        slopes.append(pull(jnp.ones_like(inner))[0].astype(BF16))
        outer = outer + dot_nt(acts[f], outer_w[f])
    second_n, second_r = norm_stats(outer)
    output = (second_n * second_gain + second_bias).astype(BF16)[:length]
    ct = pad_rows(cotangent.astype(F32), rows)
    grad_second = norm_back(ct, second_n, second_r, second_gain)
    grad_gain_two = jnp.sum(ct * second_n, 0)
    grad_bias_two = jnp.sum(ct, 0)
    grad_outer_bias = jnp.sum(grad_second, 0)
    grad_low = grad_second.astype(BF16)
    grad_first = grad_second
    ffn_grads, inner_sums = [], []
    for f in range(ffn):
        grad_inner = dot_nn(grad_low, outer_w[f]) * slopes[f].astype(F32)
        inner_sums.append(jnp.sum(grad_inner, 0))
        grad_inner = grad_inner.astype(BF16)
        grad_first = grad_first + dot_nt(grad_inner, inner_w[f])
        grad_inner_w = dot_tn(first_low, grad_inner).astype(BF16)
        grad_outer_w = dot_tn(grad_low, acts[f]).astype(BF16)
        ffn_grads.append(
            jnp.concatenate(
                [
                    grad_inner_w.reshape(dp, inner_rows, columns),
                    grad_outer_w.reshape(dp, inner_rows, columns),
                ],
                1,
            )
        )
    ffn_shard = scatter_all(jnp.stack(ffn_grads, 1))

    grad_attn = norm_back(grad_first, first_n, first_r, first_gain)
    grad_gain_one = jnp.sum(grad_first * first_n, 0)
    grad_bias_one = jnp.sum(grad_first, 0)
    grad_attn_low = grad_attn.astype(BF16)
    grad_output_w = dot_tn(mixed, grad_attn_low).astype(BF16)
    grad_mixed = dot_nt(grad_attn_low, output_full).astype(BF16)
    early = [grad_gain_one, grad_bias_one, grad_outer_bias, grad_gain_two, grad_bias_two]
    early = sum_all(jnp.concatenate(early + inner_sums).reshape(-1, 128)).reshape(-1)

    ds, grad_q, grad_k, grad_v = attend_back(qkv, grad_mixed, probs)
    grad_hidden = (
        grad_attn
        + dot_nt(grad_q, query_full)
        + dot_nt(grad_k, key_full)
        + dot_nt(grad_v, value_full)
    )
    text_grad = grad_hidden[:text_len]
    grad_tokens = lax.dot_general(
        picker,
        grad_hidden[text_len:length],
        (((0,), (0,)), ((), ())),
        precision=lax.Precision.HIGHEST,
        preferred_element_type=F32,
    ).astype(BF16)
    grad_proj = dot_tn(bn_rows, grad_tokens).astype(BF16)
    grad_bn = dot_nt(grad_tokens, proj_full)
    bn_sums = jnp.stack([jnp.sum(grad_bn, 0), jnp.sum(grad_bn * normalized, 0)])
    bn_sums = sum_all(bn_sums)
    partials = [grad_output_w] + [dot_tn(lowered, g).astype(BF16) for g in (grad_q, grad_k, grad_v)]
    partials = [grad_proj] + partials
    shard_rows = [p.shape[0] // devices for p in partials]
    tail = scatter_all(
        jnp.concatenate([p.reshape(dp, ffn, -1, width) for p in partials], 2)
    )
    begins = [sum(shard_rows[:n]) for n in range(len(shard_rows))]
    shards = [tail[b : b + n] for b, n in zip(begins, shard_rows)]

    sums = sum_all(table_sums(rel_bucket, x_bucket, y_bucket, ds, levels))[:, :heads]
    shift_grad, scale_grad = bn_sums[0], bn_sums[1]
    visual_grad = (
        bn_scale * inv_std * (grad_bn - shift_grad / count - normalized * scale_grad / count)
    )
    return (
        output,
        text_grad,
        visual_grad,
        scale_grad,
        shift_grad,
        shards[0],
        shards[2],
        shards[3],
        shards[4],
        shards[1],
        sums[: levels[0]],
        sums[levels[0] : levels[0] + levels[1]],
        sums[levels[0] + levels[1] :],
        early[:width],
        early[width : 2 * width],
        ffn_shard[:inner_rows],
        early[5 * width :],
        ffn_shard[inner_rows:].T,
        early[2 * width : 3 * width],
        early[3 * width : 4 * width],
        early[4 * width : 5 * width],
    )


def solution(mesh):
    rows = P(ALL, None)
    cube = P(ALL, None, None)
    return jax.shard_map(
        on_device,
        mesh=mesh,
        in_specs=(rows,) * 4
        + (cube,) * 3
        + (P(),) * 2
        + (rows,) * 5
        + (P(),) * 5
        + (P("dp", "ffn"), P(), P("ffn", "dp"))
        + (P(),) * 3
        + (rows,),
        out_specs=(rows,) * 3
        + (P(),) * 2
        + (rows,) * 5
        + (P(),) * 5
        + (P("dp", "ffn"), P(), P("ffn", "dp"))
        + (P(),) * 3,
        check_vma=False,
    )
```

time: 1260 us -> 651 us (0.52)
  waiting for transfers between devices: 430 us -> 101 us
  matrix products: 381 us -> 58.2 us
  Pallas kernels: 0 us -> 296 us
  blocking collectives: 258 us -> 0 us
  starting transfers between devices: 5.89 us -> 73.7 us
  local copies, waits for them, and re-layouts: 111 us -> 57.6 us
    dot_general x47 -> x39, matrix products: 381 us -> 58.2 us  [the longest x13 25.1 us: dot_tn(): lax.dot_general(a, b, (((0,), (0,)), ((), ())), preferred_element_type=F32)]
    pallas_call x0 -> x5, Pallas kernels: none -> 296 us  [the longest x1 205 us: place_blocks(): pl.pallas_call(functools.partial(place_kernel, layout), in_specs=[pl.Bloc...]
    reduce_scatter x7 -> x0, waiting for transfers between devices: 251 us -> none  [the longest x1 120 us: on_device(): lax.psum_scatter(grad_proj, ('dp', 'ffn'), scatter_dimension=0, tiled=True)]
    all_gather x9 -> x1, waiting for transfers between devices: 174 us -> 0.01 us  [on_device(): late = lax.all_gather(late, ALL, axis=0).reshape((dp, ffn) + late.shape)]
    unnamed x2 -> x0, blocking collectives: 132 us -> none
    psum x3 -> x0, blocking collectives: 126 us -> none  [the longest x1 43.8 us: on_device(): lax.psum((tables_grad[0], tables_grad[1], tables_grad[2], grad_gain_one,...]
    ppermute x0 -> x48, waiting for transfers between devices: none -> 101 us  [the longest x31 74.5 us: send_dp(): return lax.ppermute(values, 'dp', [(i, i ^ bits) for i in range(size)])]
    ppermute x0 -> x48, starting transfers between devices: none -> 73.7 us  [the longest x31 27.3 us: send_dp(): return lax.ppermute(values, 'dp', [(i, i ^ bits) for i in range(size)])]
  transfers between devices with their start and end apart: 18 -> 49, of which waited for: 8 -> 20; matrix products, arithmetic and copies ran while one was open for 45% -> 10% of each run, Pallas kernels for 0% -> 43%
where the time goes in v1:
time: 651 us; the launch traced here: 641 us
  Pallas kernels  296 us (45%)
  waiting for transfers between devices  101 us (16%)
  starting transfers between devices  73.7 us (11%)
  matrix products  58.2 us (9%)
  local copies, waits for them, and re-layouts  57.6 us (9%)
  other arithmetic  36.9 us (6%)
  between operations  17.7 us (3%)
    pallas_call x1, Pallas kernels, place_blocks(): pl.pallas_call(functools.partial(place_kernel, layout), in_specs=[pl.Bloc...  205 us
    ppermute x31, waiting for transfers between devices, send_dp(): return lax.ppermute(values, 'dp', [(i, i ^ bits) for i in range(size)])  74.5 us
    pallas_call x1, Pallas kernels, table_sums(): pl.pallas_call(functools.partial(table_kernel, length, step, levels), gri...  42 us
    unnamed x163, local copies, waits for them, and re-layouts  29.9 us
    ppermute x31, starting transfers between devices, send_dp(): return lax.ppermute(values, 'dp', [(i, i ^ bits) for i in range(size)])  27.3 us
    ppermute x8, starting transfers between devices, swap_ffn(): return lax.ppermute(values, 'ffn', [(i, i ^ bits) for i in range(size)])  26.6 us
    dot_general x13, matrix products, dot_tn(): lax.dot_general(a, b, (((0,), (0,)), ((), ())), preferred_element_type=F32)  25.1 us
    ppermute x9, waiting for transfers between devices, send_ffn(): lax.ppermute(values, 'ffn', [(i, (i + shift) % size) for i in range(size)])  22.4 us
  transfers between devices with their start and end apart: 49, of which 20 were waited for; matrix products, arithmetic and copies ran while one was open for 10% of the time, Pallas kernels for 43%

profile of v1, /device:TPU:0, one launch (start us, length us, event | category | flops | bytes accessed | tf_op | source)
XLA Modules:
  0.0 641.1 jit_solution(12805133188184473144)
XLA Ops:
  30.0 6.4 %collective-permute-done.6 = bf16[136,768]{1,0:T(8,128)(2,1)S(1)} collective-permute-done((bf16[136,768]{1,0:T(8,128)(2,1)S(1)}, bf16[136,768]{1,0:T(8,128)(2,1)S(1)}, u32[]{:S(2)}, u32[]{:S(2)}) %collective-permute-start.6) | collective-permute-done | bytes 208928 | tf_op jit(solution)/shard_map/ppermute | solution.py:42
  39.8 7.4 %collective-permute-start.3 = (f32[2,2048]{1,0:T(2,128)S(1)}, f32[2,2048]{1,0:T(2,128)S(1)}, u32[]{:S(2)}, u32[]{:S(2)}) collective-permute-start(f32[2,2048]{1,0:T(2,128)S(1)} %pad_maximum_fusion.18), channel_id=1, source_target_pairs={{0,1},{1,0},{2,3},{3,2},{4,5},{5,4},{6,7},{7,6},{8,9},{9,8},{10,11... | collective-permute-start | bytes 49160 | tf_op jit(solution)/shard_map/ppermute | solution.py:47
  49.5 12.4 %collective-permute-done.11.refs_4_ = bf16[544,768]{1,0:T(8,128)(2,1)S(1)} collective-permute-done((bf16[544,768]{1,0:T(8,128)(2,1)S(1)}, bf16[544,768]{1,0:T(8,128)(2,1)S(1)}, u32[]{:S(2)}, u32[]{:S(2)}) %collective-permute-start.11) | collective-permute-done | bytes 835616 | tf_op jit(solution)/shard_map/ppermute | solution.py:37
  64.3 4.9 collective-permute-done.9.refs_2_
  70.7 6.8 %collective-permute-start.4 = (f32[2,2048]{1,0:T(2,128)}, f32[2,2048]{1,0:T(2,128)}, u32[]{:S(2)}, u32[]{:S(2)}) collective-permute-start(f32[2,2048]{1,0:T(2,128)} %pad_maximum_fusion.19), channel_id=1, source_target_pairs={{0,2},{1,3},{2,0},{3,1},{4,6},{5,7},{6,4},{7,5},{8,10},{9,11},{10,... | collective-permute-start | bytes 49160 | tf_op jit(solution)/shard_map/ppermute | solution.py:47
  84.5 17.3 %bias_words.1.w_ref = s32[6,576,640]{2,1,0:T(8,128)S(1)} custom-call(s32[1,561,561]{2,1,0:T(8,128)S(1)} %copy.62.rel_ref, s32[1,561,561]{2,1,0:T(8,128)S(1)} %copy.63.x_ref, s32[1,561,561]{2,1,0:T(8,128)S(1)} %copy-done.6, s32[16,128]{1,0:T(8,128)S(1)} %pad_add_fusion.tab_ref), custom_call_target="tpu_custom_call" | custom-call | bytes 60000000 | tf_op jit(solution)/shard_map/bias_words/pallas_call | solution.py:202
  101.9 3.3 copy-done.1
  116.5 204.5 %place_blocks.1 = (bf16[768,768]{1,0:T(8,128)(2,1)}, bf16[768,768]{1,0:T(8,128)(2,1)}, bf16[768,768]{1,0:T(8,128)(2,1)}, bf16[2048,768]{1,0:T(8,128)(2,1)}) custom-call(s32[8]{0:T(128)} %stack.100.place_ref, bf16[544,768]{1,0:T(8,128)(2,1)} %copy-done.21, bf16[544,768]{1,0:T(8,128)(2,1)} %copy-done.40, bf16[544,768]{1,0:T(8,128)(2,1)} %copy-done.25, ...), custom_call_target="tpu_custom_call" | custom-call | tf_op jit(solution)/shard_map/place_blocks/pallas_call | solution.py:167
  328.5 14.4 %attend.1 = (bf16[12,576,576]{2,1,0:T(8,128)(2,1)}, bf16[576,768]{1,0:T(8,128)(2,1)S(1)}) custom-call(f32[1]{0:T(128)} %bitcast.21.unit_ref, bf16[576,2304]{1,0:T(8,128)(2,1)S(1)} %pad_maximum_fusion.q_ref.k_ref.v_ref, bf16[576,2304]{1,0:T(8,128)(2,1)S(1)} %pad_maximum_fusion.q_ref.k_ref.v_ref, bf16[576,2304]{1,0:T(8,128)(2,1)S(1)} %pad_maximum_fusion.q_ref.k_ref.v_ref, ...), custom_call_target="tpu_custom_call" | custom-call | flops 2038431744 | bytes 40000000 | tf_op jit(solution)/shard_map/attend/pallas_call | solution.py:248
  345.2 7.1 %slice_bitcast_fusion.1 = (bf16[4,8,96,768]{3,2,0,1:T(8,128)(2,1)S(1)}, bf16[4,8,96,768]{3,2,0,1:T(8,128)(2,1)}) fusion(bf16[8,4,216,768]{3,2,1,0:T(8,128)(2,1)} %bitcast.234), kind=kLoop, calls=%fused_computation.6 | loop fusion | bytes 18874368 | tf_op jit(solution)/shard_map/transpose | solution.py:514
  403.1 17.5 %attend_back.1 = (bf16[12,576,640]{2,1,0:T(8,128)(2,1)}, bf16[576,768]{1,0:T(8,128)(2,1)S(1)}, bf16[576,768]{1,0:T(8,128)(2,1)S(1)}, bf16[576,768]{1,0:T(8,128)(2,1)S(1)}) custom-call(bf16[576,2304]{1,0:T(8,128)(2,1)} %copy-done, bf16[576,2304]{1,0:T(8,128)(2,1)} %copy-done, bf16[576,2304]{1,0:T(8,128)(2,1)} %copy-done, ...), custom_call_target="tpu_custom_call" | custom-call | flops 4076863488 | bytes 40000000 | tf_op jit(solution)/shard_map/attend_back/pallas_call | solution.py:305
  436.5 5.9 maximum_maximum_fusion
  445.0 3.8 copy-done.10
  451.3 42.0 %table_sums.1 = f32[160,16]{1,0:T(8,128)S(1)} custom-call(s32[1,561,561]{2,1,0:T(8,128)S(1)} %copy-done.3, s32[1,561,561]{2,1,0:T(8,128)S(1)} %copy-done.5, s32[1,561,561]{2,1,0:T(8,128)S(1)} %copy-done.7, bf16[12,576,640]{2,1,0:T(8,128)(2,1)S(1)} %bitcast.227), custom_call_target="tpu_custom_call" | custom-call | bytes 120000000 | tf_op jit(solution)/shard_map/table_sums/pallas_call | solution.py:368
  504.0 3.5 collective-permute-start.33
  528.1 4.6 fusion.1
  537.9 3.9 fusion
  542.8 8.1 %collective-permute-done.25 = bf16[4,80,768]{2,1,0:T(8,128)(2,1)} collective-permute-done((bf16[4,80,768]{2,1,0:T(8,128)(2,1)}, bf16[4,80,768]{2,1,0:T(8,128)(2,1)}, u32[]{:S(2)}, u32[]{:S(2)}) %collective-permute-start.25) | collective-permute-done | bytes 491552 | tf_op jit(solution)/shard_map/ppermute | solution.py:37
  557.1 6.3 collective-permute-done.43
  565.1 24.5 %collective-permute-done.41 = bf16[4,96,768]{2,1,0:T(8,128)(2,1)S(1)} collective-permute-done((bf16[4,96,768]{2,1,0:T(8,128)(2,1)S(1)}, bf16[4,96,768]{2,1,0:T(8,128)(2,1)S(1)}, u32[]{:S(2)}, u32[]{:S(2)}) %collective-permute-start.41) | collective-permute-done | bytes 589856 | tf_op jit(solution)/shard_map/ppermute | solution.py:37
  597.8 6.0 collective-permute-done.44
  610.5 5.0 collective-permute-start.46
  615.5 10.8 %collective-permute-done.28 = bf16[160,768]{1,0:T(8,128)(2,1)S(1)} collective-permute-done((bf16[160,768]{1,0:T(8,128)(2,1)S(1)}, bf16[160,768]{1,0:T(8,128)(2,1)S(1)}, u32[]{:S(2)}, u32[]{:S(2)}) %collective-permute-start.28) | collective-permute-done | bytes 245792 | tf_op jit(solution)/shard_map/ppermute | solution.py:42
  627.9 5.1 collective-permute-done.46
  (410 shorter events, 191.5 us)
Async XLA Ops:
  7.2 336.6 %all-gather.3.cloned.1.call-start = ((), (), s32[]{:S(2)}) async-start(), calls=%async_computation | async-start | bytes 10948608 | tf_op jit(solution)/shard_map/all_gather | solution.py:457
  12.3 17.6 %collective-permute-start.7 = (bf16[136,768]{1,0:T(8,128)(2,1)S(1)}, bf16[136,768]{1,0:T(8,128)(2,1)S(1)}, u32[]{:S(2)}, u32[]{:S(2)}) collective-permute-start(bf16[136,768]{1,0:T(8,128)(2,1)S(1)} %constant_dynamic-update-slice_fusion), channel_id=1, source_target_pairs={{0,1},{1,2},{2,3},{3,0},{4,5},{5,6},{6,7},{7,4},{8,9},{9,10},{10,1... | collective-permute-start | bytes 626696 | tf_op jit(solution)/shard_map/ppermute | solution.py:42
  15.4 21.0 %collective-permute-start.6 = (bf16[136,768]{1,0:T(8,128)(2,1)S(1)}, bf16[136,768]{1,0:T(8,128)(2,1)S(1)}, u32[]{:S(2)}, u32[]{:S(2)}) collective-permute-start(bf16[136,768]{1,0:T(8,128)(2,1)S(1)} %constant_dynamic-update-slice_fusion), channel_id=1, source_target_pairs={{0,2},{1,3},{2,0},{3,1},{4,6},{5,7},{6,4},{7,5},{8,10},{9,11},{10,... | collective-permute-start | bytes 626696 | tf_op jit(solution)/shard_map/ppermute | solution.py:42
  18.0 18.4 %collective-permute-start.5 = (bf16[136,768]{1,0:T(8,128)(2,1)S(1)}, bf16[136,768]{1,0:T(8,128)(2,1)S(1)}, u32[]{:S(2)}, u32[]{:S(2)}) collective-permute-start(bf16[136,768]{1,0:T(8,128)(2,1)S(1)} %constant_dynamic-update-slice_fusion), channel_id=1, source_target_pairs={{0,3},{1,0},{2,1},{3,2},{4,7},{5,4},{6,5},{7,6},{8,11},{9,8},{10,9... | collective-permute-start | bytes 626696 | tf_op jit(solution)/shard_map/ppermute | solution.py:42
  36.7 25.2 %collective-permute-start.11 = (bf16[544,768]{1,0:T(8,128)(2,1)S(1)}, bf16[544,768]{1,0:T(8,128)(2,1)S(1)}, u32[]{:S(2)}, u32[]{:S(2)}) collective-permute-start(bf16[544,768]{1,0:T(8,128)(2,1)S(1)} %pad_maximum_fusion.5.refs_0_), channel_id=1, source_target_pairs={{0,16},{4,20},{8,24},{12,28},{16,0},{20,4},{24,8},{28,12},{1,17},{... | collective-permute-start | bytes 2506760 | tf_op jit(solution)/shard_map/ppermute | solution.py:37
  38.2 31.0 %collective-permute-start.9 = (bf16[544,768]{1,0:T(8,128)(2,1)S(1)}, bf16[544,768]{1,0:T(8,128)(2,1)S(1)}, u32[]{:S(2)}, u32[]{:S(2)}) collective-permute-start(bf16[544,768]{1,0:T(8,128)(2,1)S(1)} %pad_maximum_fusion.5.refs_0_), channel_id=1, source_target_pairs={{0,8},{4,12},{8,0},{12,4},{16,24},{20,28},{24,16},{28,20},{1,9},{5... | collective-permute-start | bytes 2506760 | tf_op jit(solution)/shard_map/ppermute | solution.py:37
  62.7 44.4 %collective-permute-start.14 = (bf16[272,768]{1,0:T(8,128)(2,1)}, bf16[272,768]{1,0:T(8,128)(2,1)}, u32[]{:S(2)}, u32[]{:S(2)}) collective-permute-start(bf16[272,768]{1,0:T(8,128)(2,1)} %slice.349), channel_id=1, source_target_pairs={{0,8},{4,12},{8,0},{12,4},{16,24},{20,28},{24,16},{28,20},{1,9},{5... | collective-permute-start | bytes 1253384 | tf_op jit(solution)/shard_map/ppermute | solution.py:37
  70.1 37.6 %collective-permute-start.13 = (bf16[272,768]{1,0:T(8,128)(2,1)}, bf16[272,768]{1,0:T(8,128)(2,1)}, u32[]{:S(2)}, u32[]{:S(2)}) collective-permute-start(bf16[272,768]{1,0:T(8,128)(2,1)} %slice.348), channel_id=1, source_target_pairs={{0,16},{4,20},{8,24},{12,28},{16,0},{20,4},{24,8},{28,12},{1,17},{... | collective-permute-start | bytes 1253384 | tf_op jit(solution)/shard_map/ppermute | solution.py:37
  70.7 35.7 %collective-permute-start.4 = (f32[2,2048]{1,0:T(2,128)}, f32[2,2048]{1,0:T(2,128)}, u32[]{:S(2)}, u32[]{:S(2)}) collective-permute-start(f32[2,2048]{1,0:T(2,128)} %pad_maximum_fusion.19), channel_id=1, source_target_pairs={{0,2},{1,3},{2,0},{3,1},{4,6},{5,7},{6,4},{7,5},{8,10},{9,11},{10,... | collective-permute-start | bytes 49160 | tf_op jit(solution)/shard_map/ppermute | solution.py:47
  432.9 95.2 %collective-permute-start.22 = (bf16[4,4,160,768]{3,2,1,0:T(8,128)(2,1)}, bf16[4,4,160,768]{3,2,1,0:T(8,128)(2,1)}, u32[]{:S(2)}, u32[]{:S(2)}) collective-permute-start(bf16[4,4,160,768]{3,2,1,0:T(8,128)(2,1)} %dynamic-slice_bitcast_fusion.1), channel_id=1, source_target_pairs={{0,4},{4,0},{8,12},{12,8},{16,20},{20,16},{24,28},{28,24},{1,5},{5... | collective-permute-start | bytes 11796488 | tf_op jit(solution)/shard_map/ppermute | solution.py:37
  448.8 89.1 %collective-permute-start.40 = (bf16[4,4,192,768]{3,2,0,1:T(8,128)(2,1)}, bf16[4,4,192,768]{3,2,0,1:T(8,128)(2,1)}, u32[]{:S(2)}, u32[]{:S(2)}) collective-permute-start(bf16[4,4,192,768]{3,2,0,1:T(8,128)(2,1)} %dynamic-slice_bitcast_fusion), channel_id=1, source_target_pairs={{0,4},{4,0},{8,12},{12,8},{16,20},{20,16},{24,28},{28,24},{1,5},{5... | collective-permute-start | bytes 14155784 | tf_op jit(solution)/shard_map/ppermute | solution.py:37
  450.8 45.5 %collective-permute-start.17 = (f32[2,2048]{1,0:T(2,128)S(1)}, f32[2,2048]{1,0:T(2,128)S(1)}, u32[]{:S(2)}, u32[]{:S(2)}) collective-permute-start(f32[2,2048]{1,0:T(2,128)S(1)} %pad_maximum_fusion.20), channel_id=1, source_target_pairs={{0,4},{4,0},{8,12},{12,8},{16,20},{20,16},{24,28},{28,24},{1,5},{5... | collective-permute-start | bytes 49160 | tf_op jit(solution)/shard_map/ppermute | solution.py:37
  526.3 65.9 %collective-permute-start.39 = (f32[54,128]{1,0:T(8,128)S(1)}, f32[54,128]{1,0:T(8,128)S(1)}, u32[]{:S(2)}, u32[]{:S(2)}) collective-permute-start(f32[54,128]{1,0:T(8,128)S(1)} %add.647), channel_id=1, source_target_pairs={{0,2},{1,3},{2,0},{3,1},{4,6},{5,7},{6,4},{7,5},{8,10},{9,11},{10,... | collective-permute-start | bytes 82952 | tf_op jit(solution)/shard_map/ppermute | solution.py:47
  535.7 18.5 %collective-permute-start.23 = (bf16[4,80,768]{2,1,0:T(8,128)(2,1)}, bf16[4,80,768]{2,1,0:T(8,128)(2,1)}, u32[]{:S(2)}, u32[]{:S(2)}) collective-permute-start(bf16[4,80,768]{2,1,0:T(8,128)(2,1)} %get-tuple-element.124), channel_id=1, source_target_pairs={{0,16},{4,20},{8,24},{12,28},{16,0},{20,4},{24,8},{28,12},{1,17},{... | collective-permute-start | bytes 1474568 | tf_op jit(solution)/shard_map/ppermute | solution.py:37
  542.2 21.3 %collective-permute-start.43 = (bf16[4,96,768]{2,1,0:T(8,128)(2,1)S(1)}, bf16[4,96,768]{2,1,0:T(8,128)(2,1)S(1)}, u32[]{:S(2)}, u32[]{:S(2)}) collective-permute-start(bf16[4,96,768]{2,1,0:T(8,128)(2,1)S(1)} %get-tuple-element.120), channel_id=1, source_target_pairs={{0,8},{4,12},{8,0},{12,4},{16,24},{20,28},{24,16},{28,20},{1,9},{5... | collective-permute-start | bytes 1769480 | tf_op jit(solution)/shard_map/ppermute | solution.py:37
  552.2 41.3 %collective-permute-start.26 = (bf16[4,160,768]{2,1,0:T(8,128)(2,1)S(1)}, bf16[4,160,768]{2,1,0:T(8,128)(2,1)S(1)}, u32[]{:S(2)}, u32[]{:S(2)}) collective-permute-start(bf16[4,160,768]{2,1,0:T(8,128)(2,1)S(1)} %pad_maximum_fusion.4), channel_id=1, source_target_pairs={{0,16},{4,20},{8,24},{12,28},{16,0},{20,4},{24,8},{28,12},{1,17},{... | collective-permute-start | bytes 2949128 | tf_op jit(solution)/shard_map/ppermute | solution.py:37
  553.6 36.0 %collective-permute-start.41 = (bf16[4,96,768]{2,1,0:T(8,128)(2,1)S(1)}, bf16[4,96,768]{2,1,0:T(8,128)(2,1)S(1)}, u32[]{:S(2)}, u32[]{:S(2)}) collective-permute-start(bf16[4,96,768]{2,1,0:T(8,128)(2,1)S(1)} %get-tuple-element.119), channel_id=1, source_target_pairs={{0,16},{4,20},{8,24},{12,28},{16,0},{20,4},{24,8},{28,12},{1,17},{... | collective-permute-start | bytes 1769480 | tf_op jit(solution)/shard_map/ppermute | solution.py:37
  555.5 37.9 %collective-permute-start.24 = (bf16[4,160,768]{2,1,0:T(8,128)(2,1)S(1)}, bf16[4,160,768]{2,1,0:T(8,128)(2,1)S(1)}, u32[]{:S(2)}, u32[]{:S(2)}) collective-permute-start(bf16[4,160,768]{2,1,0:T(8,128)(2,1)S(1)} %pad_maximum_fusion.3), channel_id=1, source_target_pairs={{0,8},{4,12},{8,0},{12,4},{16,24},{20,28},{24,16},{28,20},{1,9},{5... | collective-permute-start | bytes 2949128 | tf_op jit(solution)/shard_map/ppermute | solution.py:37
  563.7 40.1 %collective-permute-start.44 = (bf16[4,192,768]{2,1,0:T(8,128)(2,1)S(1)}, bf16[4,192,768]{2,1,0:T(8,128)(2,1)S(1)}, u32[]{:S(2)}, u32[]{:S(2)}) collective-permute-start(bf16[4,192,768]{2,1,0:T(8,128)(2,1)S(1)} %pad_maximum_fusion.2), channel_id=1, source_target_pairs={{0,16},{4,20},{8,24},{12,28},{16,0},{20,4},{24,8},{28,12},{1,17},{... | collective-permute-start | bytes 3538952 | tf_op jit(solution)/shard_map/ppermute | solution.py:37
  594.6 21.0 %collective-permute-start.29 = (bf16[160,768]{1,0:T(8,128)(2,1)S(1)}, bf16[160,768]{1,0:T(8,128)(2,1)S(1)}, u32[]{:S(2)}, u32[]{:S(2)}) collective-permute-start(bf16[160,768]{1,0:T(8,128)(2,1)S(1)} %get-tuple-element.122), channel_id=1, source_target_pairs={{0,3},{1,0},{2,1},{3,2},{4,7},{5,4},{6,5},{7,6},{8,11},{9,8},{10,9... | collective-permute-start | bytes 737288 | tf_op jit(solution)/shard_map/ppermute | solution.py:42
  597.8 28.6 %collective-permute-start.28 = (bf16[160,768]{1,0:T(8,128)(2,1)S(1)}, bf16[160,768]{1,0:T(8,128)(2,1)S(1)}, u32[]{:S(2)}, u32[]{:S(2)}) collective-permute-start(bf16[160,768]{1,0:T(8,128)(2,1)S(1)} %get-tuple-element.123), channel_id=1, source_target_pairs={{0,2},{1,3},{2,0},{3,1},{4,6},{5,7},{6,4},{7,5},{8,10},{9,11},{10,... | collective-permute-start | bytes 737288 | tf_op jit(solution)/shard_map/ppermute | solution.py:42
  606.6 21.3 %collective-permute-start.45 = (bf16[192,768]{1,0:T(8,128)(2,1)S(1)}, bf16[192,768]{1,0:T(8,128)(2,1)S(1)}, u32[]{:S(2)}, u32[]{:S(2)}) collective-permute-start(bf16[192,768]{1,0:T(8,128)(2,1)S(1)} %get-tuple-element.116), channel_id=1, source_target_pairs={{0,1},{1,2},{2,3},{3,0},{4,5},{5,6},{6,7},{7,4},{8,9},{9,10},{10,1... | collective-permute-start | bytes 884744 | tf_op jit(solution)/shard_map/ppermute | solution.py:42
  607.6 20.3 %collective-permute-start.47 = (bf16[192,768]{1,0:T(8,128)(2,1)S(1)}, bf16[192,768]{1,0:T(8,128)(2,1)S(1)}, u32[]{:S(2)}, u32[]{:S(2)}) collective-permute-start(bf16[192,768]{1,0:T(8,128)(2,1)S(1)} %get-tuple-element.117), channel_id=1, source_target_pairs={{0,3},{1,0},{2,1},{3,2},{4,7},{5,4},{6,5},{7,6},{8,11},{9,8},{10,9... | collective-permute-start | bytes 884744 | tf_op jit(solution)/shard_map/ppermute | solution.py:42
  610.5 22.5 %collective-permute-start.46 = (bf16[192,768]{1,0:T(8,128)(2,1)S(1)}, bf16[192,768]{1,0:T(8,128)(2,1)S(1)}, u32[]{:S(2)}, u32[]{:S(2)}) collective-permute-start(bf16[192,768]{1,0:T(8,128)(2,1)S(1)} %get-tuple-element.118), channel_id=1, source_target_pairs={{0,2},{1,3},{2,0},{3,1},{4,6},{5,7},{6,4},{7,5},{8,10},{9,11},{10,... | collective-permute-start | bytes 884744 | tf_op jit(solution)/shard_map/ppermute | solution.py:42
  (100 other events, 1484.3 us)
Sparse Core Ops, SparseCore 0:
  10.9 106.6 all-gather.2
